TPU v7x, 128 devices: a whole 4x4x4 slice. The times are simulated.
128 devices in a mesh: dp: 32 (over x, y, core), mp: 4 (over z).
Axes of the slice: x: 4, y: 4, z: 4, core: 2. Of those that a mesh axis runs over, the one named last changes fastest.
Arguments:
- id_lists: int32 [8, 39, 8192], P(None, None, 'dp'), may hold values from 0 to 1023
- id_counts: int32 [39, 8192], P(None, 'dp'), may hold values from 1 to 8, as said below
- embed_rows: bfloat16 [32768, 10], P('dp'), may hold values from -6 to 6
- logit_grad: bfloat16 [8192], P('dp'), may hold values from -12 to 12
- bilinear: float32 [10, 10], replicated, may hold values from -2 to 2
- bilinear_momentum: float32 [10, 10], replicated, may hold values from -56 to 56
- bilinear_average: float32 [10, 10], replicated, may hold values from -2 to 2
- squeezer: float32 [39, 13], replicated, may hold values from -3 to 3
- squeezer_momentum: float32 [39, 13], replicated, may hold values from -5 to 5
- squeezer_average: float32 [39, 13], replicated, may hold values from -3 to 3
- exciter: float32 [13, 39], replicated, may hold values from -4 to 4
- exciter_momentum: float32 [13, 39], replicated, may hold values from -5 to 5
- exciter_average: float32 [13, 39], replicated, may hold values from -4 to 4
- pairwise: float32 [20, 741, 400], P('mp'), may hold values from -0.046875 to 0.046875
- pairwise_momentum: float32 [20, 741, 400], P('mp'), may hold values from -2.5 to 2.5
- pairwise_average: float32 [20, 741, 400], P('mp'), may hold values from -0.046875 to 0.046875
- fieldwise: float32 [10, 39, 400], P(None, None, 'mp'), may hold values from -0.3125 to 0.3125
- fieldwise_momentum: float32 [10, 39, 400], P(None, None, 'mp'), may hold values from -4 to 4
- fieldwise_average: float32 [10, 39, 400], P(None, None, 'mp'), may hold values from -0.3125 to 0.3125
- hidden: float32 [2, 400, 400], P(None, None, 'mp'), may hold values from -0.3125 to 0.3125
- hidden_momentum: float32 [2, 400, 400], P(None, None, 'mp'), may hold values from -4 to 4
- hidden_average: float32 [2, 400, 400], P(None, None, 'mp'), may hold values from -0.3125 to 0.3125
- biases: float32 [3, 400], P(None, 'mp'), may hold values from -3 to 3
- biases_momentum: float32 [3, 400], P(None, 'mp'), may hold values from -10 to 10
- biases_average: float32 [3, 400], P(None, 'mp'), may hold values from -3 to 3
- readout: float32 [400], P('mp'), may hold values from -0.3125 to 0.3125
- readout_momentum: float32 [400], P('mp'), may hold values from -256 to 256
- readout_average: float32 [400], P('mp'), may hold values from -0.3125 to 0.3125
- offset: float32 [1], replicated, may hold values from -6 to 6
- offset_momentum: float32 [1], replicated, may hold values from -1024 to 1024
- offset_average: float32 [1], replicated, may hold values from -6 to 6
Outputs:
- logits: float32 [8192], P('dp')
- embed_grad: float32 [10, 39, 8192], P(None, None, 'dp')
- bilinear_velocity: float32 [10, 10], replicated
- bilinear_smoothed: float32 [10, 10], replicated
- bilinear_updated: float32 [10, 10], replicated
- squeezer_velocity: float32 [39, 13], replicated
- squeezer_smoothed: float32 [39, 13], replicated
- squeezer_updated: float32 [39, 13], replicated
- exciter_velocity: float32 [13, 39], replicated
- exciter_smoothed: float32 [13, 39], replicated
- exciter_updated: float32 [13, 39], replicated
- pairwise_velocity: float32 [20, 741, 400], P('mp')
- pairwise_smoothed: float32 [20, 741, 400], P('mp')
- pairwise_updated: float32 [20, 741, 400], P('mp')
- fieldwise_velocity: float32 [10, 39, 400], P(None, None, 'mp')
- fieldwise_smoothed: float32 [10, 39, 400], P(None, None, 'mp')
- fieldwise_updated: float32 [10, 39, 400], P(None, None, 'mp')
- hidden_velocity: float32 [2, 400, 400], P(None, None, 'mp')
- hidden_smoothed: float32 [2, 400, 400], P(None, None, 'mp')
- hidden_updated: float32 [2, 400, 400], P(None, None, 'mp')
- biases_velocity: float32 [3, 400], P(None, 'mp')
- biases_smoothed: float32 [3, 400], P(None, 'mp')
- biases_updated: float32 [3, 400], P(None, 'mp')
- readout_velocity: float32 [400], P('mp')
- readout_smoothed: float32 [400], P('mp')
- readout_updated: float32 [400], P('mp')
- offset_velocity: float32 [1], replicated
- offset_smoothed: float32 [1], replicated
- offset_updated: float32 [1], replicated
Inputs may be any that keep to these rules, and one draw needn't show every extreme that they name: `id_lists`: an id of event n indexes the 1024 rows fetched for block n // 256. `id_counts`: slots at or past the count are padding and are ignored.
All inputs are finite; a program needn't handle non-finite values.
Results may differ from a plain program's by a relative error of at most 0.018.
Values may be sent and summed in bfloat16 or wider, within the bound.
A program may use at most 128 MiB of HBM per device.

v0:
```python
import jax
import jax.numpy as jnp
import numpy as np
from jax import lax
from jax.experimental import pallas as pl
from jax.experimental.pallas import tpu as pltpu
from jax.sharding import PartitionSpec as P

MOMENTUM = 0.9
RATE = 0.01
FAST_RATE = 0.05
DECAY = 0.8
HIGHEST = lax.Precision.HIGHEST
F32 = jnp.float32
LOW = jnp.bfloat16
MESH = pl.DeviceIdType.MESH
MIB = 1024 * 1024

EMB = 10
FIELDS = 39
FPAD = 40
REDUCED = 13
UNITS = 400
ZROWS = 112
ZPARTS = ((0, 64), (64, 48))
UDEV = 100
SLOTS = 8
BATCH = 256
FETCH = 1024
PAIRS = 741
PPAD = 768
HALF = 384
ROWS = 5
TILES = 416
HALVES = TILES // 2
CHUNKS = (112, 96)
KTILES = 75
BUFFERS = 3
AUX = 38
SMALL = 16
STEPS = 4095


def dot(left, right, contract, precision=None):
    return lax.dot_general(
        left, right, ((contract[0], contract[1]), ((), ())),
        precision=precision, preferred_element_type=F32,
    )


def nn(left, right, precision=None):
    return dot(left, right, ((1,), (0,)), precision)


def nt(left, right, precision=None):
    return dot(left, right, ((1,), (1,)), precision)


def tn(left, right, precision=None):
    return dot(left, right, ((0,), (0,)), precision)


def in_hbm(arrays):
    return tuple(pltpu.with_memory_space_constraint(array, pltpu.HBM) for array in arrays)


def nesterov(weight, momentum, average, grad, step_rate):
    velocity = MOMENTUM * momentum + grad
    updated = weight - step_rate * (grad + MOMENTUM * velocity)
    smoothed = DECAY * average + (1.0 - DECAY) * updated
    return (velocity, smoothed, updated)


def pool(ids_ref, count_ref, rows_ref, counts, table, out_ref, between):
    rows = rows_ref[...].astype(F32)
    largest = jnp.maximum(jnp.max(jnp.abs(rows), keepdims=True), 1e-30)
    fixed = jnp.round(rows * (STEPS / largest)).astype(jnp.int32) + (STEPS + 1)
    for chunk in range(8):
        part = fixed[:, 128 * chunk:128 * (chunk + 1)]
        for k in range(EMB // 2):
            table[k, chunk:chunk + 1, :] = part[2 * k:2 * k + 1, :] * 65536 + part[2 * k + 1:2 * k + 2, :]
    counts[0:FIELDS, :] = count_ref[...]
    counts[FIELDS:FPAD, :] = jnp.ones((1, BATCH), jnp.int32)
    ids_ref[FIELDS] = jnp.full((SLOTS, BATCH), 8 * FETCH, jnp.int32)
    sublane = lax.broadcasted_iota(jnp.int32, (8, 128), 0)
    unit = largest * (1.0 / STEPS)

    def group(g, carry):
        fields = pl.ds(pl.multiple_of(8 * g, 8), 8)
        for h in range(2):
            lanes = slice(128 * h, 128 * (h + 1))
            live = counts[fields, lanes]
            found = [[] for _ in range(EMB // 2)]
            for row in range(8):
                ids = jnp.where(live[row:row + 1, :] > sublane, ids_ref[8 * g + row, :, lanes], 8 * FETCH)
                totals = [None] * (EMB // 2)
                for slot in range(SLOTS):
                    wide = jnp.broadcast_to(ids[slot:slot + 1, :], (8, 128))
                    lane = wide & 127
                    hit = (wide >> 7) == sublane
                    for k in range(EMB // 2):
                        value = jnp.take_along_axis(table[k], lane, axis=1, mode="promise_in_bounds")
                        value = jnp.where(hit, value, 0)
                        totals[k] = value if totals[k] is None else totals[k] + value
                for k in range(EMB // 2):
                    found[k].append(jnp.sum(totals[k], axis=0, keepdims=True))
            factor = unit / live.astype(F32)
            for k in range(EMB // 2):
                both = jnp.concatenate(found[k], axis=0)
                for part, word in enumerate(((both >> 16) & 65535, both & 65535)):
                    total = (word - (STEPS + 1) * live).astype(F32)
                    out_ref[2 * k + part, fields, lanes] = (total * factor).astype(LOW).astype(F32)
        return carry

    lax.fori_loop(0, 2, group, 0)
    between()
    lax.fori_loop(2, FPAD // 8, group, 0)
    out_ref[:, FPAD - 8:FPAD, :] = jnp.where(
        lax.broadcasted_iota(jnp.int32, (EMB, 8, BATCH), 1) == 7, 0.0, out_ref[:, FPAD - 8:FPAD, :]
    )


def gate_of(before):
    return 0.5 + 0.5 * jnp.tanh(0.5 * before)


def silu_slope(before, gate):
    return gate * (1.0 + before * (1.0 - gate))


def softplus(value):
    return jnp.maximum(value, 0.0) + jnp.log1p(jnp.exp(-jnp.abs(value)))


def two_terms(value):
    high = value.astype(LOW)
    return high, (value - high.astype(F32)).astype(LOW)


def split(value):
    high = value.astype(LOW).astype(F32)
    return jnp.concatenate([high, value - high], axis=0).astype(LOW)


def step_kernel(*refs):
    hbm, pairs_in, refs = refs[:20], refs[20:23], refs[23:]
    gout_ref, small_ref, egrad_ref, logit_ref, *pairs_out = refs[:7]
    loaded, refs = refs[7:27], refs[27:]
    pair_ref = pairs_out[0]
    (
        ids_ref, count_ref, rows_ref, hidden_ref,
        field_ref, bias_ref, readout_ref, grad_ref, squ_ref, exc_ref,
        first_ref, second_ref, first_t_ref, second_t_ref, place_ref, place_t_ref, same_ref, rows_of_ref, cols_of_ref, bil_ref,
    ) = loaded
    (
        emb_ref, counts, table, w_low, w_turned, left, right, feats, feats_peer, source, scale_s, sq_s, z1_s, z2_s,
        squ_pad, exc_pad, fpad, fplaced, fplaced_t, hid_all, vec_all, hid_full, hid_turned,
        pre_part, rs_in, pre_full, gf, gf_peer,
        acc, box1, box2, aux, aux_in,
        dsrc, eterm, zsend, zrecv, zsend2, zrecv2, zsend3, zrecv3, small_z, small_x, small_y, small_c,
        load_sem, pair_sem, hid_send, hid_recv, vec_send, vec_recv, twin_sem, feat_sem,
        rsz_send, rsz_recv, agz_send, agz_recv,
        gf_sem, aux_sem, red_send, red_recv, own_sem, gat_send, gat_recv, core_send, core_recv,
        zs_send, zs_recv, smz_send, smz_recv, smx_send, smx_recv, smy_send, smy_recv, smc_sem,
    ) = refs
    dp = lax.axis_index("dp")
    me = lax.axis_index("mp")
    core = dp % 2
    yy = (dp // 2) % 4
    xx = dp // 8

    def at_dp(x, y, c):
        return (x * 4 + y) * 2 + c

    rings = (
        [((xx + off) % 4, at_dp((xx + off) % 4, yy, core)) for off in (1, 3, 2)],
        [((yy + off) % 4, at_dp(xx, (yy + off) % 4, core)) for off in (1, 3, 2)],
    )
    places = (xx, yy)
    twin = at_dp(xx, yy, 1 - core)
    peers = [(me + off) % 4 for off in (1, 3, 2)]
    stream = me // 2
    columns = (me % 2) * ROWS
    half = ((me + 1) // 2) % 2
    near = me + 1 - 2 * (me % 2)
    cross = 3 - me

    def remote(src, dst, send, recv, **where):
        return pltpu.make_async_remote_copy(
            src_ref=src, dst_ref=dst, send_sem=send, recv_sem=recv, device_id=where, device_id_type=MESH
        )

    targets = (ids_ref.at[pl.ds(0, FIELDS)],) + loaded[1:]
    loads = [pltpu.make_async_copy(src, dst, load_sem.at[n]) for n, (src, dst) in enumerate(zip(hbm, targets))]
    for copy in loads:
        copy.start()
    pair_loads = [
        pltpu.make_async_copy(src, dst, pair_sem.at[n]) for n, (src, dst) in enumerate(zip(pairs_in, pairs_out))
    ]
    for copy in pair_loads:
        copy.start()
    barrier = pltpu.get_barrier_semaphore()
    for peer in peers:
        pl.semaphore_signal(barrier, inc=1, device_id={"mp": peer}, device_id_type=MESH)
    for dev in [dev for ring in rings for _, dev in ring] + [twin]:
        pl.semaphore_signal(barrier, inc=1, device_id={"dp": dev}, device_id_type=MESH)

    lanes_me = pl.ds(pl.multiple_of(128 * me, 128), 128)
    hid_copies = []
    for n, peer in enumerate(peers):
        mine = hid_all.at[core, :, lanes_me]
        hid_copies.append(remote(mine, mine, hid_send.at[n], hid_recv.at[n], mp=peer))
        mine = vec_all.at[:, lanes_me]
        hid_copies.append(remote(mine, mine, vec_send.at[n], vec_recv.at[n], mp=peer))

    def share_hidden():
        for copy in loads[3:]:
            copy.wait()
        fpad[...] = jnp.zeros_like(fpad)
        fpad[:, 0:UDEV] = hidden_ref[core]
        hid_all[core, :, lanes_me] = fpad[...].astype(LOW)
        fpad[0:8, :] = jnp.zeros((8, 128), F32)
        fpad[0:3, 0:UDEV] = bias_ref[...]
        fpad[3:4, 0:UDEV] = readout_ref[...].astype(LOW).astype(F32)
        vec_all[:, lanes_me] = fpad[0:8, :]
        pl.semaphore_wait(barrier, 10)
        for copy in hid_copies:
            copy.start()

    for copy in loads[:3]:
        copy.wait()
    pool(ids_ref, count_ref, rows_ref, counts, table, emb_ref, share_hidden)

    squ_pad[...] = jnp.zeros_like(squ_pad)
    squ_pad[0:REDUCED, 0:FIELDS] = squ_ref[...]
    exc_pad[...] = jnp.zeros_like(exc_pad)
    exc_pad[0:REDUCED, 0:FIELDS] = exc_ref[...]
    squeezer = squ_pad[:, 0:FPAD]
    exciter = exc_pad[:, 0:FPAD]
    emb = emb_ref[...]
    squeezed = jnp.sum(emb, axis=0) * (1.0 / EMB)
    z1 = nn(squeezer, squeezed, HIGHEST)
    z2 = tn(exciter, z1 * gate_of(z1), HIGHEST)
    scales = softplus(z2)
    sq_s[...] = squeezed
    z1_s[...] = z1
    z2_s[...] = z2
    scale_s[...] = scales
    factor = jnp.where(stream == 0, jnp.ones_like(scales), scales)
    for k in range(EMB):
        source[k] = emb_ref[k] * factor

    for k in range(ROWS):
        projected = source[0] * bil_ref[0, columns + k]
        for l in range(1, EMB):
            projected = projected + source[l] * bil_ref[l, columns + k]
        left_k = nn(first_ref[...], split(projected))
        right_k = nn(second_ref[...], split(source[columns + k]))
        left[k] = left_k.astype(LOW)
        right[k] = right_k.astype(LOW)
        feats[k] = (left_k * right_k).astype(LOW)
    feat_copy = remote(
        feats.at[:, pl.ds(pl.multiple_of(HALF * (1 - core), HALF), HALF), :], feats_peer,
        feat_sem.at[0], feat_sem.at[1], dp=twin,
    )
    feat_copy.start()
    fpad[0:8, :] = jnp.zeros((8, 128), F32)
    for k in range(EMB):
        fpad[FPAD * k:FPAD * k + FIELDS, 0:UDEV] = field_ref[k]
        fpad[FPAD * k + FIELDS:FPAD * (k + 1), :] = jnp.zeros((1, 128), F32)
    field_low = fpad[...].astype(LOW)
    place_own = place_ref[lanes_me, :]
    fplaced_t[...] = nt(place_t_ref[:, lanes_me], field_low).astype(LOW)
    emb_low = emb.reshape(EMB * FPAD, BATCH).astype(LOW)
    pre = nn(fplaced_t[...], emb_low)
    pair_loads[0].wait()
    for k in range(ROWS):
        w_low[k, :, 640:PPAD] = jnp.zeros((UNITS, PPAD - 640), LOW)
        w_low[k, :, 0:PAIRS] = pair_ref[k].astype(LOW)
        pre = pre + nn(w_low[k], feats[k])
    pre_part[0:UNITS, :] = pre.astype(LOW)
    pre_part[UNITS:4 * ZROWS, :] = jnp.zeros((4 * ZROWS - UNITS, BATCH), LOW)

    rs_copies = []
    for part, (low_row, count) in enumerate(ZPARTS):
        for n, peer in enumerate(peers):
            rows = pl.ds(pl.multiple_of(ZROWS * peer + low_row, 16), count)
            box = rs_in.at[n, pl.ds(low_row, count)]
            rs_copies.append(remote(pre_part.at[rows], box, rsz_send.at[part, n], rsz_recv.at[part, n], mp=peer))
            rs_copies[-1].start()
    for copy in hid_copies:
        copy.wait()
    layer = hid_all.at[core]
    hid_twin = remote(layer, layer, twin_sem.at[0], twin_sem.at[1], dp=twin)
    hid_twin.start()
    fplaced[...] = nn(field_low, place_own).astype(LOW)
    ag_copies = []
    for part, (low_row, count) in enumerate(ZPARTS):
        for copy in rs_copies[3 * part:3 * part + 3]:
            copy.wait()
        own_rows = pl.ds(pl.multiple_of(ZROWS * me + low_row, 16), count)
        total = pre_part[own_rows, :].astype(F32)
        for n in range(3):
            total = total + rs_in[n, low_row:low_row + count].astype(F32)
        pre_full[own_rows, :] = total.astype(LOW)
        mine = pre_full.at[own_rows]
        for n, peer in enumerate(peers):
            ag_copies.append(remote(mine, mine, agz_send.at[part, n], agz_recv.at[part, n], mp=peer))
            ag_copies[-1].start()

    hid_twin.wait()
    for layer in range(2):
        hid_full[layer] = nn(hid_all[layer], place_ref[...]).astype(LOW)
        hid_turned[layer] = nt(place_t_ref[...], hid_all[layer]).astype(LOW)
    vec_rows = nn(vec_all[...], place_ref[...].astype(F32), HIGHEST)
    vec_cols = nt(place_t_ref[...].astype(F32), vec_all[...], HIGHEST)
    for copy in ag_copies:
        copy.wait()

    pre_first = pre_full[0:UNITS, :].astype(F32) + vec_cols[:, 0:1]
    gate_first = gate_of(pre_first)
    act_first = (pre_first * gate_first).astype(LOW)
    pre_second = nn(hid_turned[0], act_first) + vec_cols[:, 1:2]
    gate_second = gate_of(pre_second)
    act_second = (pre_second * gate_second).astype(LOW)
    pre_third = nn(hid_turned[1], act_second) + vec_cols[:, 2:3]
    gate_third = gate_of(pre_third)
    act_third = (pre_third * gate_third).astype(LOW)
    upstream = grad_ref[...].astype(F32).reshape(1, BATCH)
    grad_third = ((vec_cols[:, 3:4] * upstream) * silu_slope(pre_third, gate_third)).astype(LOW)
    grad_second = (nn(hid_full[1], grad_third) * silu_slope(pre_second, gate_second)).astype(LOW)
    grad_first = (nn(hid_full[0], grad_second) * silu_slope(pre_first, gate_first)).astype(LOW)
    gf[...] = grad_first
    gf_copy = remote(gf, gf_peer, gf_sem.at[0], gf_sem.at[1], dp=twin)
    gf_copy.start()

    first_mine = nn(place_own, grad_first).astype(LOW)
    second_mine = nn(place_own, grad_second).astype(LOW)
    third_mine = nn(place_own, grad_third).astype(LOW)
    aux[0:25] = nt(emb_low, first_mine).astype(LOW).reshape(25, 16, 128)
    aux[25:50] = nt(act_first, second_mine).astype(LOW).reshape(25, 16, 128)
    aux[50:75] = nt(act_second, third_mine).astype(LOW).reshape(25, 16, 128)
    aux[75] = jnp.zeros((16, 128), LOW)
    aux_copy = remote(
        aux.at[pl.ds(AUX * (1 - core), AUX)], aux_in, aux_sem.at[0], aux_sem.at[1], dp=twin
    )
    aux_copy.start()

    feat_copy.wait()
    own_half = pl.ds(pl.multiple_of(HALF * core, HALF), HALF)
    gf_copy.wait()
    for k in range(ROWS):
        grad = (nt(gf[...], feats[k, own_half, :]) + nt(gf_peer[...], feats_peer[k])).astype(LOW)
        tiles = [grad[:, 128 * j:128 * (j + 1)].reshape(25, 16, 128) for j in range(3)]
        acc[KTILES * k:KTILES * (k + 1)] = jnp.stack(tiles, axis=1).reshape(KTILES, 16, 128)
    acc[KTILES * ROWS + AUX:TILES] = jnp.zeros((TILES - KTILES * ROWS - AUX, 16, 128), LOW)

    offsets = (0, CHUNKS[0])
    starts = [[HALVES * h + offsets[c] for c in range(2)] for h in range(2)]

    def size_of(t, c):
        return CHUNKS[c] // (4, 16)[t]

    def box_of(t, h, n, c):
        return (box1, box2)[t].at[h, n, pl.ds(offsets[c] // (4, 16)[t], size_of(t, c))]

    def reduce_send(t, c):
        size = size_of(t, c)
        copies = []
        for n in range(3):
            for h in range(2):
                place, dev = rings[(h + t) % 2][n]
                src = acc.at[pl.ds(starts[h][c] + place * size, size)]
                copies.append(
                    remote(src, box_of(t, h, n, c), red_send.at[t, h, c, n], red_recv.at[t, h, c, n], dp=dev)
                )
                copies[-1].start()
        for h in range(2):
            starts[h][c] = starts[h][c] + places[(h + t) % 2] * size
        return copies

    def reduce_add(t, c, copies):
        for copy in copies:
            copy.wait()
        for h in range(2):
            keep = pl.ds(starts[h][c], size_of(t, c))
            total = acc[keep].astype(F32)
            for n in range(3):
                total = total + box_of(t, h, n, c)[...].astype(F32)
            acc[keep] = total.astype(LOW)

    own_copies = []
    core_copies = []

    def pass_on(h, c, slot, start, count):
        where = gout_ref.at[core, pl.ds(start, count)]
        copy = remote(where, where, core_send.at[h, c, slot], core_recv.at[h, c, slot], dp=twin)
        copy.start()
        core_copies.append(copy)

    def gather_send(t, c):
        size = size_of(t, c)
        copies = []
        for n in range(3):
            for h in range(2):
                _, dev = rings[(h + t) % 2][n]
                where = gout_ref.at[core, pl.ds(starts[h][c], size)]
                src = acc.at[pl.ds(starts[h][c], size)] if t == 1 else where
                copy = remote(src, where, gat_send.at[t, h, c, n], gat_recv.at[t, h, c, n], dp=dev)
                copy.start()
                sender = rings[(h + t) % 2][(1, 0, 2)[n]][0]
                came = starts[h][c] + (sender - places[(h + t) % 2]) * size
                copies.append((copy, h, n, came))
        for h in range(2):
            if t == 1:
                where = pl.ds(starts[h][c], size)
                own = pltpu.make_async_copy(acc.at[where], gout_ref.at[core, where], own_sem.at[h, c])
                own.start()
                own_copies.append(own)
            starts[h][c] = starts[h][c] - places[(h + t) % 2] * size
        return copies

    def gather_wide(c, copies):
        for copy, _, _, _ in copies:
            copy.wait()
        for own in own_copies[2 * c:2 * c + 2]:
            own.wait()
        wide = gather_send(0, c)
        for h in range(2):
            pass_on(h, c, 3, starts[h][c] + places[h] * size_of(0, c), size_of(0, c))
        return wide

    def gather_end(c, copies):
        for copy, h, n, came in copies:
            copy.wait()
            pass_on(h, c, n, came, size_of(0, c))

    moving = [reduce_send(0, 0)]
    aux_copy.wait()
    aux_mine = aux[pl.ds(AUX * core, AUX)].astype(F32) + aux_in[...].astype(F32)
    acc[KTILES * ROWS:KTILES * ROWS + AUX] = aux_mine.astype(LOW)
    moving.append(reduce_send(0, 1))
    act_mine = nn(place_own, act_third).astype(LOW)
    ones = jnp.ones((16, BATCH), LOW)
    upstream_rows = jnp.broadcast_to(upstream, (16, BATCH)).astype(LOW)
    row_iota = lax.broadcasted_iota(jnp.int32, (16, 128), 0)
    vec_grads = jnp.where(row_iota == 0, nt(ones, first_mine), 0.0)
    vec_grads = vec_grads + jnp.where(row_iota == 1, nt(ones, second_mine), 0.0)
    vec_grads = vec_grads + jnp.where(row_iota == 2, nt(ones, third_mine), 0.0)
    vec_grads = vec_grads + jnp.where(row_iota == 3, nt(upstream_rows, act_mine), 0.0)

    dprojected = []
    dchosen = []
    for k in range(ROWS):
        w_turned[k] = jnp.transpose(w_low[k])
        dfeat = nn(w_turned[k], gf[...])
        dprojected.append(nn(first_t_ref[...], (dfeat * right[k].astype(F32)).astype(LOW)))
        dchosen.append(nn(second_t_ref[...], (dfeat * left[k].astype(F32)).astype(LOW)))
    for l in range(EMB):
        total = dprojected[0] * bil_ref[l, columns]
        for k in range(1, ROWS):
            total = total + dprojected[k] * bil_ref[l, columns + k]
        dsrc[l] = total
    for k in range(ROWS):
        dsrc[columns + k] = dsrc[columns + k] + dchosen[k]
    eterm[...] = nn(fplaced[...], gf[...]).reshape(EMB, FPAD, BATCH)
    lanes_away = pl.ds(pl.multiple_of(128 * (1 - half), 128), 128)
    lanes_own = pl.ds(pl.multiple_of(128 * half, 128), 128)
    zsend[0] = dsrc[:, :, lanes_away].reshape(EMB * FPAD, 128).astype(LOW)
    zsend[1] = eterm[:, :, lanes_away].reshape(EMB * FPAD, 128).astype(LOW)
    z_copies = [remote(zsend.at[n], zrecv.at[n], zs_send.at[n], zs_recv.at[n], mp=near) for n in range(2)]
    for copy in z_copies:
        copy.start()
    source_high, source_rest = two_terms(source[...].reshape(EMB * FPAD, BATCH))
    dproj_high, dproj_rest = two_terms(jnp.concatenate(dprojected, axis=0))
    products = nt(source_high, dproj_high) + nt(source_high, dproj_rest) + nt(source_rest, dproj_high)
    products = products * same_ref[...].astype(F32)
    bil_rows = nn(nn(rows_of_ref[...].astype(F32), products, HIGHEST), cols_of_ref[me % 2].astype(F32), HIGHEST)
    bil_rows = jnp.where(row_iota == 15, jnp.sum(upstream) * 0.25, bil_rows)
    reduce_add(0, 0, moving[0])
    moving[0] = reduce_send(1, 0)

    z_copies[0].wait()
    back = dsrc[:, :, lanes_own] + zrecv[0].astype(F32).reshape(EMB, FPAD, 128)
    emb_half = emb_ref[:, :, lanes_own]
    z1 = z1_s[:, lanes_own]
    z2 = z2_s[:, lanes_own]
    dscale = jnp.sum(back * emb_half, axis=0)
    dz2 = dscale * gate_of(z2)
    gate = gate_of(z1)
    dexciter = nt(z1 * gate, dz2, HIGHEST)
    dz1 = nn(exciter, dz2, HIGHEST) * silu_slope(z1, gate)
    dsqueezer = nt(dz1, sq_s[:, lanes_own], HIGHEST)
    weighted = jnp.where(stream == 0, jnp.zeros((1, 1), F32), jnp.ones((1, 1), F32))

    small_z[me] = jnp.concatenate([dsqueezer * weighted, dexciter * weighted, bil_rows[:, 0:128 - 2 * FPAD]], axis=1)
    small = []
    for n, peer in enumerate(peers):
        small.append(remote(small_z.at[me], small_z.at[me], smz_send.at[n], smz_recv.at[n], mp=peer))
        small[n].start()
    dsqueezed = tn(squeezer, dz1, HIGHEST) * (1.0 / EMB)
    through = back * scale_s[:, lanes_own][None] + dsqueezed[None]
    z_copies[1].wait()
    term = eterm[:, :, lanes_own] + zrecv[1].astype(F32).reshape(EMB, FPAD, 128)
    mine = term + jnp.where(stream == 0, back, through)
    zsend2[...] = mine.reshape(EMB * FPAD, 128).astype(LOW)
    z_copy = remote(zsend2, zrecv2, zs_send.at[2], zs_recv.at[2], mp=cross)
    z_copy.start()

    reduce_add(0, 1, moving[1])
    moving[1] = reduce_send(1, 1)
    for copy in small:
        copy.wait()
    small_x[xx, 0:SMALL] = small_z[0] + small_z[1] + small_z[2] + small_z[3]
    small_x[xx, SMALL:SMALL + 8] = vec_grads[0:8]
    small = []
    for n, (_, dev) in enumerate(rings[0]):
        small.append(remote(small_x.at[xx], small_x.at[xx], smx_send.at[n], smx_recv.at[n], dp=dev))
        small[n].start()
    reduce_add(1, 0, moving[0])
    moving[0] = gather_send(1, 0)
    reduce_add(1, 1, moving[1])
    moving[1] = gather_send(1, 1)
    for copy in small:
        copy.wait()
    small_y[yy] = small_x[0] + small_x[1] + small_x[2] + small_x[3]
    small = []
    for n, (_, dev) in enumerate(rings[1]):
        small.append(remote(small_y.at[yy], small_y.at[yy], smy_send.at[n], smy_recv.at[n], dp=dev))
        small[n].start()
    moving[0] = gather_wide(0, moving[0])
    moving[1] = gather_wide(1, moving[1])
    logit_ref[...] = nn(vec_rows.astype(LOW), act_third)
    z_copy.wait()
    whole = (zsend2[...].astype(F32) + zrecv2[...].astype(F32)).astype(LOW)
    zsend3[...] = whole
    z_copy = remote(zsend3, zrecv3, zs_send.at[3], zs_recv.at[3], mp=near)
    z_copy.start()
    egrad_ref[:, :, lanes_own] = whole.reshape(EMB, FPAD, 128)
    gather_end(0, moving[0])
    for copy in small:
        copy.wait()
    small_c[core] = small_y[0] + small_y[1] + small_y[2] + small_y[3]
    small = remote(small_c.at[core], small_c.at[core], smc_sem.at[0], smc_sem.at[1], dp=twin)
    small.start()
    z_copy.wait()
    egrad_ref[:, :, lanes_away] = zrecv3[...].reshape(EMB, FPAD, 128)
    gather_end(1, moving[1])
    small.wait()
    small_ref[...] = small_c[0] + small_c[1]
    for copy in core_copies + pair_loads[1:]:
        copy.wait()


def step(id_lists, id_counts, embed_rows, pair_set, fieldwise, hidden, biases, readout, logit_grad, bilinear, squeezer, exciter):
    first_index, second_index = np.triu_indices(FIELDS, 1)
    first = np.zeros((PPAD, FPAD), np.float32)
    second = np.zeros((PPAD, FPAD), np.float32)
    first[np.arange(PAIRS), first_index] = 1.0
    second[np.arange(PAIRS), second_index] = 1.0
    place = np.zeros((512, UNITS), np.float32)
    unit = np.arange(UNITS)
    place[128 * (unit // UDEV) + unit % UDEV, unit] = 1.0
    pair_field = np.arange(EMB * FPAD)
    same = (pair_field[:, None] % FPAD == pair_field[None, :ROWS * FPAD] % FPAD).astype(np.float32)
    rows_of = (np.arange(16)[:, None] == pair_field[None, :] // FPAD).astype(np.float32)
    cols_of = np.stack([
        (pair_field[:ROWS * FPAD, None] // FPAD + ROWS * part == np.arange(128)[None, :]).astype(np.float32) for part in range(2)
    ])
    constants = (
        np.concatenate([first, first], axis=1), np.concatenate([second, second], axis=1), first.T, second.T, place, place.T,
        same, rows_of, cols_of,
    )
    constants = [jnp.asarray(value, LOW) for value in constants]
    small_operands = (
        id_lists.transpose(1, 0, 2), id_counts, embed_rows.T, hidden,
        fieldwise, biases, readout.reshape(1, UDEV), logit_grad, squeezer.T, exciter,
        *constants, bilinear,
    )
    vmem = pl.BlockSpec(memory_space=pltpu.VMEM)
    hbm = pl.BlockSpec(memory_space=pltpu.HBM)
    anywhere = pl.BlockSpec(memory_space=pl.ANY)
    low = lambda *shape: pltpu.VMEM(shape, LOW)
    full = lambda *shape: pltpu.VMEM(shape, F32)
    dma = lambda *shape: pltpu.SemaphoreType.DMA(shape)
    return pl.pallas_call(
        step_kernel,
        out_shape=(
            pltpu.VMEM((2, TILES, 16, 128), LOW),
            jax.ShapeDtypeStruct((SMALL + 8, 128), F32),
            jax.ShapeDtypeStruct((EMB, FPAD, BATCH), LOW),
            jax.ShapeDtypeStruct((8, BATCH), F32),
        ) + (pltpu.VMEM(pair_set[0].shape, F32),) * 3,
        in_specs=[hbm] * 23,
        out_specs=(anywhere, vmem, vmem, vmem) + (vmem,) * 3,
        scratch_shapes=[
            pltpu.VMEM((FPAD, SLOTS, BATCH), jnp.int32),
            *(pltpu.VMEM(array.shape, array.dtype) for array in small_operands[1:-1]),
            pltpu.SMEM((EMB, EMB), F32),
            full(EMB, FPAD, BATCH), pltpu.VMEM((FPAD, BATCH), jnp.int32), pltpu.VMEM((EMB // 2, 8, 128), jnp.int32),
            low(ROWS, UNITS, PPAD), low(ROWS, PPAD, UNITS),
            low(ROWS, PPAD, BATCH), low(ROWS, PPAD, BATCH), low(ROWS, PPAD, BATCH), low(ROWS, HALF, BATCH),
            full(EMB, FPAD, BATCH), full(FPAD, BATCH), full(FPAD, BATCH), full(16, BATCH), full(FPAD, BATCH),
            full(16, 128), full(16, 128), full(EMB * FPAD, 128), low(EMB * FPAD, UNITS), low(UNITS, EMB * FPAD),
            low(2, UNITS, 512), full(8, 512), low(2, UNITS, UNITS), low(2, UNITS, UNITS),
            low(4 * ZROWS, BATCH), low(3, ZROWS, BATCH), low(4 * ZROWS, BATCH), low(UNITS, BATCH), low(UNITS, BATCH),
            low(TILES, 16, 128), low(2, 3, HALVES // 4, 16, 128), low(2, 3, HALVES // 16, 16, 128),
            low(2 * AUX, 16, 128), low(AUX, 16, 128),
            full(EMB, FPAD, BATCH), full(EMB, FPAD, BATCH),
            low(2, EMB * FPAD, 128), low(2, EMB * FPAD, 128), low(EMB * FPAD, 128), low(EMB * FPAD, 128),
            low(EMB * FPAD, 128), low(EMB * FPAD, 128),
            full(4, SMALL, 128), full(4, SMALL + 8, 128), full(4, SMALL + 8, 128), full(2, SMALL + 8, 128),
            dma(20), dma(3), dma(3), dma(3), dma(3), dma(3), dma(2), dma(2),
            dma(2, 3), dma(2, 3), dma(2, 3), dma(2, 3),
            dma(2), dma(2), dma(2, 2, 2, 3), dma(2, 2, 2, 3), dma(2, 2), dma(2, 2, 2, 3), dma(2, 2, 2, 3),
            dma(2, 2, 4), dma(2, 2, 4),
            dma(4), dma(4), dma(3), dma(3), dma(3), dma(3), dma(3), dma(3), dma(2),
        ],
        compiler_params=pltpu.CompilerParams(
            collective_id=0, has_side_effects=True, vmem_limit_bytes=32 * MIB
        ),
        name="step",
    )(*in_hbm(small_operands), *in_hbm(pair_set))


def update_kernel(grads, small, egrad, logit, weight, momentum, average, *refs):
    inputs, refs = refs[:24], refs[24:]
    logits_out, egrad_out = refs[:2]
    pair_outs, outputs, refs = refs[2:5], refs[5:29], refs[29:]
    held, refs = refs[:24], refs[24:]
    logits_held, egrad_held, pair_held, in_sem, out_sem, pair_sem = refs

    loads = [pltpu.make_async_copy(src, dst, in_sem.at[n]) for n, (src, dst) in enumerate(zip(inputs, held))]
    for copy in loads:
        copy.start()

    def put(which, at, grad, rate):
        weight, momentum, average = held[3 * which:3 * which + 3]
        values = nesterov(weight[at], momentum[at], average[at], grad, rate)
        for ref, value in zip((weight, momentum, average), values):
            ref[at] = value

    def small_ones():
        for copy in loads:
            copy.wait()
        tiles = slice(KTILES * ROWS, KTILES * ROWS + AUX)
        whole = jnp.concatenate([grads[0, tiles], grads[1, tiles]], axis=0).astype(F32).reshape(2 * AUX * 16, 128)
        for k in range(EMB):
            put(0, (k,), whole[FPAD * k:FPAD * k + FIELDS, 0:UDEV], RATE)
        for layer in range(2):
            put(1, (layer,), whole[UNITS * (layer + 1):UNITS * (layer + 2), 0:UDEV], RATE)
        everything = (slice(None), slice(None))
        offset_weight = held[12][...]
        put(2, everything, small[SMALL:SMALL + 3, 0:UDEV], FAST_RATE)
        put(3, everything, small[SMALL + 3:SMALL + 4, 0:UDEV], RATE)
        put(4, everything, small[15:16, 2 * FPAD:2 * FPAD + 1], RATE)
        put(5, everything, small[0:EMB, 2 * FPAD:2 * FPAD + EMB], RATE)
        put(6, everything, small[0:REDUCED, 0:FIELDS], FAST_RATE)
        put(7, everything, small[0:REDUCED, FPAD:FPAD + FIELDS], FAST_RATE)
        logits_held[...] = logit[3:4, :] + offset_weight
        for k in range(EMB):
            egrad_held[k] = egrad[k, :, :].astype(F32)[0:FIELDS]
        ends = zip((logits_held, egrad_held) + tuple(held), (logits_out, egrad_out) + tuple(outputs))
        ends = [pltpu.make_async_copy(src, dst, out_sem.at[n]) for n, (src, dst) in enumerate(ends)]
        for copy in ends:
            copy.start()
        return ends

    stores = []
    for k in range(ROWS):
        slot = k % BUFFERS
        if k >= BUFFERS:
            for copy in stores[3 * (k - BUFFERS):3 * (k - BUFFERS + 1)]:
                copy.wait()
        for c in range(2):
            for j in range(3):
                first = HALF * c + 128 * j
                last = min(first + 128, PAIRS)
                tiles = [grads[c, KTILES * k + 3 * r + j] for r in range(UNITS // 16)]
                grad = jnp.concatenate(tiles, axis=0).astype(F32)[:, 0:last - first]
                at = (k, slice(None), slice(first, last))
                values = nesterov(weight[at], momentum[at], average[at], grad, RATE)
                for n, value in enumerate(values):
                    pair_held[slot, n, :, first:last] = value
        for n in range(3):
            stores.append(pltpu.make_async_copy(pair_held.at[slot, n], pair_outs[n].at[k], pair_sem.at[slot, n]))
            stores[-1].start()
        if k == 1:
            lasts = small_ones()
    for copy in lasts + stores[3 * (ROWS - BUFFERS):]:
        copy.wait()


def update(grads, small, egrad, logit, sets):
    vmem = pl.BlockSpec(memory_space=pltpu.VMEM)
    hbm = pl.BlockSpec(memory_space=pltpu.HBM)
    pair, others = sets[0], [array for arrays in sets[1:] for array in arrays]
    shapes = [(1, BATCH), (EMB, FIELDS, BATCH)] + [array.shape for array in pair] + [array.shape for array in others]
    return pl.pallas_call(
        update_kernel,
        in_specs=[vmem] * 7 + [hbm] * 24,
        out_specs=[hbm] * 29,
        out_shape=[jax.ShapeDtypeStruct(shape, F32) for shape in shapes],
        scratch_shapes=[
            *(pltpu.VMEM(array.shape, F32) for array in others),
            pltpu.VMEM((1, BATCH), F32), pltpu.VMEM((EMB, FIELDS, BATCH), F32),
            pltpu.VMEM((BUFFERS, 3, UNITS, PAIRS), F32),
            pltpu.SemaphoreType.DMA((24,)), pltpu.SemaphoreType.DMA((26,)), pltpu.SemaphoreType.DMA((BUFFERS, 3)),
        ],
        compiler_params=pltpu.CompilerParams(vmem_limit_bytes=18 * MIB),
        name="update",
    )(grads, small, egrad, logit, *pair, *in_hbm(others[:12]), *others[12:15], *in_hbm(others[15:]))


def per_device(
    id_lists, id_counts, embed_rows, logit_grad,
    bilinear, bilinear_momentum, bilinear_average,
    squeezer, squeezer_momentum, squeezer_average,
    exciter, exciter_momentum, exciter_average,
    pairwise, pairwise_momentum, pairwise_average,
    fieldwise, fieldwise_momentum, fieldwise_average,
    hidden, hidden_momentum, hidden_average,
    biases, biases_momentum, biases_average,
    readout, readout_momentum, readout_average,
    offset, offset_momentum, offset_average,
):
    turn = lambda *arrays: tuple(array.swapaxes(-1, -2) for array in arrays)
    pair_set = turn(pairwise, pairwise_momentum, pairwise_average)
    grads, small, egrad, logit, *held = step(
        id_lists, id_counts, embed_rows, pair_set, fieldwise, hidden, biases, readout, logit_grad, bilinear, squeezer, exciter
    )
    row = lambda *arrays: tuple(array.reshape(1, -1) for array in arrays)
    outs = update(
        grads, small, egrad, logit,
        [
            held,
            (fieldwise, fieldwise_momentum, fieldwise_average),
            (hidden, hidden_momentum, hidden_average),
            (biases, biases_momentum, biases_average),
            row(readout, readout_momentum, readout_average),
            row(offset, offset_momentum, offset_average),
            (bilinear, bilinear_momentum, bilinear_average),
            turn(squeezer, squeezer_momentum, squeezer_average),
            (exciter, exciter_momentum, exciter_average),
        ],
    )
    logits, egrad_full = outs[0].reshape(-1), outs[1]
    pair, field, hid, bias, read, off, bil, squ, exc = (tuple(outs[2 + 3 * i:5 + 3 * i]) for i in range(9))
    flat = lambda arrays: tuple(array.reshape(-1) for array in arrays)
    return (logits, egrad_full) + bil + turn(*squ) + exc + turn(*pair) + field + hid + bias + flat(read) + flat(off)


def solution(mesh):
    whole = (P(),) * 3
    rows = (P("mp", None, None),) * 3
    units = (P(None, None, "mp"),) * 3
    vectors = (P(None, "mp"),) * 3
    line = (P("mp"),) * 3
    weights = whole + whole + whole + rows + units + units + vectors + line + whole
    return jax.shard_map(
        per_device,
        mesh=mesh,
        in_specs=(P(None, None, "dp"), P(None, "dp"), P("dp", None), P("dp")) + weights,
        out_specs=(P("dp"), P(None, None, "dp")) + weights,
        check_vma=False,
    )
```

profile of v0, /device:TPU:0, one launch (start us, length us, event | category | flops | bytes accessed | tf_op | source)
XLA Modules:
  0.0 72.7 jit_solution(1912046655113521995)
XLA Ops:
  2.6 61.6 %step.1 = (bf16[2,416,16,128]{3,2,1,0:T(8,128)(2,1)S(1)}, f32[24,128]{1,0:T(8,128)S(1)}, bf16[10,40,256]{2,1,0:T(8,128)(2,1)S(1)}, f32[8,256]{1,0:T(8,128)S(1)},...) custom-call(s32[39,8,256]{2,1,0:T(8,128)} %bitcast.33, s32[39,256]{1,0:T(8,128)} %refs_1_.2, ...), custom_call_target="tpu_custom_call" | custom-call | tf_op jit(solution)/shard_map/step/pallas_call | solution.py:586
  64.2 8.3 %update.1 = (f32[1,256]{1,0:T(1,128)}, f32[10,39,256]{2,1,0:T(8,128)}, f32[5,400,741]{2,1,0:T(8,128)}, f32[5,400,741]{2,1,0:T(8,128)}, f32[5,400,741]{2,1,0:T(8,...) custom-call(bf16[2,416,16,128]{3,2,1,0:T(8,128)(2,1)S(1)} %get-tuple, ...), custom_call_target="tpu_custom_call" | custom-call | tf_op jit(solution)/shard_map/update/pallas_call | solution.py:699
where the time goes:
time: 74.2 us; the launch traced here: 72.7 us
  Pallas kernels  69.9 us (94%)
  between operations  2.8 us (4%)
    pallas_call x1, Pallas kernels, step(): pl.pallas_call(step_kernel, out_shape=(pltpu.VMEM((2, TILES, 16, 128), LO...  61.6 us
    pallas_call x1, Pallas kernels, update(): pl.pallas_call(update_kernel, in_specs=[vmem] * 7 + [hbm] * 24, out_specs...  8.29 us

commit v1 on v0

--- a/solution.py
+++ b/solution.py
@@ -197,8 +197,6 @@
     pair_loads = [
         pltpu.make_async_copy(src, dst, pair_sem.at[n]) for n, (src, dst) in enumerate(zip(pairs_in, pairs_out))
     ]
-    for copy in pair_loads:
-        copy.start()
     barrier = pltpu.get_barrier_semaphore()
     for peer in peers:
         pl.semaphore_signal(barrier, inc=1, device_id={"mp": peer}, device_id_type=MESH)
@@ -229,6 +227,8 @@
 
     for copy in loads[:3]:
         copy.wait()
+    for copy in pair_loads:
+        copy.start()
     pool(ids_ref, count_ref, rows_ref, counts, table, emb_ref, share_hidden)
 
     squ_pad[...] = jnp.zeros_like(squ_pad)

time: 74.2 us -> 74.1 us (level)
  no operation moved by 1% of the time
where the time goes in v1:
time: 74.1 us; the launch traced here: 72.7 us
  Pallas kernels  69.9 us (94%)
  between operations  2.8 us (4%)
    pallas_call x1, Pallas kernels, step(): pl.pallas_call(step_kernel, out_shape=(pltpu.VMEM((2, TILES, 16, 128), LO...  61.6 us
    pallas_call x1, Pallas kernels, update(): pl.pallas_call(update_kernel, in_specs=[vmem] * 7 + [hbm] * 24, out_specs...  8.29 us

profile of v1, /device:TPU:0, one launch (start us, length us, event | category | flops | bytes accessed | tf_op | source)
XLA Modules:
  0.0 72.7 jit_solution(6011091397511552461)
XLA Ops:
  2.6 61.6 %step.1 = (bf16[2,416,16,128]{3,2,1,0:T(8,128)(2,1)S(1)}, f32[24,128]{1,0:T(8,128)S(1)}, bf16[10,40,256]{2,1,0:T(8,128)(2,1)S(1)}, f32[8,256]{1,0:T(8,128)S(1)},...) custom-call(s32[39,8,256]{2,1,0:T(8,128)} %bitcast.33, s32[39,256]{1,0:T(8,128)} %refs_1_.2, ...), custom_call_target="tpu_custom_call" | custom-call | tf_op jit(solution)/shard_map/step/pallas_call | solution.py:586
  64.2 8.3 %update.1 = (f32[1,256]{1,0:T(1,128)}, f32[10,39,256]{2,1,0:T(8,128)}, f32[5,400,741]{2,1,0:T(8,128)}, f32[5,400,741]{2,1,0:T(8,128)}, f32[5,400,741]{2,1,0:T(8,...) custom-call(bf16[2,416,16,128]{3,2,1,0:T(8,128)(2,1)S(1)} %get-tuple, ...), custom_call_target="tpu_custom_call" | custom-call | tf_op jit(solution)/shard_map/update/pallas_call | solution.py:699
